TPU v7x, 128 devices: a whole 4x4x4 slice. The times are simulated.
128 devices in a mesh: req: 8 (over y, core), exp: 16 (over x, z).
Axes of the slice: x: 4, y: 4, z: 4, core: 2. Of those that a mesh axis runs over, the one named last changes fastest.
Arguments:
- hidden_in: bfloat16 [16384, 2048], P(('req', 'exp')), may hold values from -6 to 6
- qkv: bfloat16 [16384, 6144], P(('req', 'exp'))
- q_gain: float32 [128], replicated, as said below
- k_gain: float32 [128], replicated, as said below
- query_pages: bfloat16 [8, 8, 128, 4096], P('req', None, None, 'exp'), may hold values from -6 to 6
- page_table: int32 [8, 8], P('req'), may hold values from 0 to 7, each once within a row
- doc_lengths: int32 [8, 32], P('req'), may hold values from 1 to 128, 2048 in all within a row
- doc_query: int32 [8, 32], P('req'), may hold values from 0 to 7
- out_weight: bfloat16 [2048, 2048], replicated, may hold values from -0.125 to 0.125
- moe_gain: float32 [2048], replicated, may hold values from 0.5 to 1.5
- routes: int32 [16384, 8], P(('req', 'exp')), may hold values from 0 to 63, all different within a row; in each aligned block of 128 rows (0 to 127, 128 to 255, ...) at most 24 rows name the same one
- route_weight: float32 [16384, 8], P(('req', 'exp')), may hold values from 0.02 to 0.25
- gate_weight: bfloat16 [128, 2048, 512], P(('req', 'exp')), may hold values from -0.125 to 0.125
- up_weight: bfloat16 [128, 2048, 512], P(('req', 'exp')), may hold values from -0.125 to 0.125
- down_weight: bfloat16 [128, 512, 2048], P(('req', 'exp')), may hold values from -0.1875 to 0.1875
- score_weight: float32 [2048], replicated, may hold values from -0.125 to 0.125
Outputs:
- layer_out: bfloat16 [16384, 2048], P(('req', 'exp'))
- doc_scores: float32 [8, 32], P('req')
Inputs may be any that keep to these rules, and one draw needn't show every extreme that they name: Among the routes of the rows of one device no expert is named more than 24 times; in every draw some device's rows name some expert exactly 24 times. `doc_lengths`: each group's 32 lengths sum to 2048; the longest of each group is exactly 128. `page_table`: each row is a permutation of the pages. `q_gain`: Positive. `k_gain`: Positive.
All inputs are finite; a program needn't handle non-finite values.
Results may differ from a plain program's by a relative error of at most 0.012.
Values may be sent and summed in bfloat16 or wider, within the bound.
A program may use at most 128 MiB of HBM per device.

v0:
```python
import jax
import jax.numpy as jnp
from jax import lax
from jax.sharding import PartitionSpec as P

HEADS = 16
HD = 128
TOP = 8
NQ = 8
PAGE = 128


eps = 1e-06
rope_base = 50000.0
neg_fill = -1e30


def padded(block, sides, width):
    for axis, dim in sides:
        count = lax.axis_size(axis)
        forward = [(i, i + 1) for i in range(count - 1)]
        backward = [(target, source) for source, target in forward]
        low = lax.ppermute(
            lax.slice_in_dim(block, block.shape[dim] - width, None, axis=dim), axis, forward
        )
        high = lax.ppermute(lax.slice_in_dim(block, 0, width, axis=dim), axis, backward)
        block = jnp.concatenate([low, block, high], axis=dim)
    return block


def rms_scale(values, gain_vec):
    mean_sq = jnp.mean(values * values, axis=-1, keepdims=True)
    return values * lax.rsqrt(mean_sq + eps) * gain_vec


def rotate(values, positions):
    half_dim = values.shape[-1] // 2
    frequency = rope_base ** (-(jnp.arange(half_dim, dtype=jnp.float32) * 2.0 / values.shape[-1]))
    angles = positions.astype(jnp.float32)[:, None] * frequency[None, :]
    cosine = jnp.cos(angles)[:, None, :]
    sine_part = jnp.sin(angles)[:, None, :]
    lower_part = values[..., :half_dim]
    upper_part = values[..., half_dim:]
    return jnp.concatenate(
        [
            lower_part * cosine - upper_part * sine_part,
            upper_part * cosine + lower_part * sine_part,
        ],
        axis=-1,
    )


def doc_table(doc_len, positions):
    doc_ends = jnp.cumsum(doc_len, dtype=jnp.int32)
    starts = doc_ends - doc_len
    doc_ids = jnp.sum(
        (positions[:, None] >= doc_ends[None, :]).astype(jnp.int32), axis=1, dtype=jnp.int32
    )
    inside = (positions >= 0) & (positions < doc_ends[-1])
    doc_ids = jnp.where(inside, doc_ids, -1)
    member = doc_ids[:, None] == jnp.arange(doc_len.shape[0], dtype=jnp.int32)[None, :]
    doc_start = jnp.sum(jnp.where(member, starts[None, :], 0), axis=1, dtype=jnp.int32)
    return (doc_ids, member, doc_start)


def page_lookup(member, doc_query, page_table):
    query_ids = jnp.sum(jnp.where(member, doc_query[None, :], 0), axis=1, dtype=jnp.int32)
    query_hit = query_ids[:, None] == jnp.arange(page_table.shape[0], dtype=jnp.int32)[None, :]
    return jnp.sum(jnp.where(query_hit, page_table[None, :], 0), axis=1, dtype=jnp.int32)


def attend(query_rows, key_rows, value_rows, visible):
    score_scale = query_rows.shape[-1] ** (-0.5)
    scores = (
        jnp.einsum("nhd,khd->hnk", query_rows, key_rows, preferred_element_type=jnp.float32)
        * score_scale
    )
    scores = jnp.where(visible[None], scores, neg_fill)
    row_max = jnp.max(scores, axis=-1)
    probs = jnp.where(visible[None], jnp.exp(scores - row_max[..., None]), 0.0)
    row_total = jnp.sum(probs, axis=-1)
    weighted = jnp.einsum(
        "hnk,khd->nhd", probs.astype(jnp.bfloat16), value_rows, preferred_element_type=jnp.float32
    )
    return (weighted, row_max.T, row_total.T)


def slot_numbers(route_flat, bin_count):
    onehot = (route_flat[:, None] == jnp.arange(bin_count, dtype=jnp.int32)[None, :]).astype(
        jnp.int32
    )
    prior_count = jnp.cumsum(onehot, axis=0, dtype=jnp.int32) - onehot
    return jnp.sum(prior_count * onehot, axis=1, dtype=jnp.int32)


def expert_piece(rows_three, gate_weight, up_weight, down_weight):
    flat_rows = rows_three.reshape(-1, rows_three.shape[-1])
    gate_act = jnp.dot(flat_rows, gate_weight[0], preferred_element_type=jnp.float32)
    up_act = jnp.dot(flat_rows, up_weight[0], preferred_element_type=jnp.float32)
    hidden_act = (jax.nn.silu(gate_act) * up_act).astype(jnp.bfloat16)
    piece_out = jnp.dot(hidden_act, down_weight[0], preferred_element_type=jnp.float32)
    return piece_out.astype(jnp.bfloat16).reshape(rows_three.shape)


def local(
    hidden_in,
    qkv,
    q_gain,
    k_gain,
    query_pages,
    page_table,
    doc_lengths,
    doc_query,
    out_weight,
    moe_gain,
    routes,
    route_weight,
    gate_weight,
    up_weight,
    down_weight,
    score_weight,
):
    tok_count = hidden_in.shape[0]
    width = hidden_in.shape[1]
    exp_count = lax.axis_size("exp")
    devices = lax.axis_size("req") * exp_count
    experts = devices // 2
    capacity = 2 * max(1, 3 * tok_count * TOP // (4 * experts))
    exp_index = lax.axis_index("exp")
    doc_len = doc_lengths[0]
    own_pos = exp_index * tok_count + jnp.arange(tok_count, dtype=jnp.int32)
    own_doc, own_member, own_start = doc_table(doc_len, own_pos)
    own_page = page_lookup(own_member, doc_query[0], page_table[0])
    rope_pos = PAGE + own_pos - own_start
    query_rows = rotate(
        rms_scale(qkv[:, :width].astype(jnp.float32).reshape(tok_count, HEADS, HD), q_gain),
        rope_pos,
    ).astype(jnp.bfloat16)
    key_rows = rotate(
        rms_scale(
            qkv[:, width : 2 * width].astype(jnp.float32).reshape(tok_count, HEADS, HD), k_gain
        ),
        rope_pos,
    ).astype(jnp.bfloat16)
    kv_local = jnp.concatenate([key_rows.reshape(tok_count, width), qkv[:, 2 * width :]], axis=1)
    window = padded(kv_local, (("exp", 0),), tok_count)
    win_pos = (exp_index - 1) * tok_count + jnp.arange(3 * tok_count, dtype=jnp.int32)
    win_doc, win_member, win_start = doc_table(doc_len, win_pos)
    win_keys = window[:, :width].reshape(3 * tok_count, HEADS, HD)
    win_values = window[:, width:].reshape(3 * tok_count, HEADS, HD)
    win_visible = win_doc[None, :] == own_doc[:, None]
    key_page = jnp.arange(NQ * PAGE, dtype=jnp.int32) // PAGE
    page_rows = lax.all_gather(query_pages[0], "exp", axis=2, tiled=True).reshape(
        NQ * PAGE, HEADS, 2, HD
    )
    all_keys = jnp.concatenate([page_rows[:, :, 0], win_keys], axis=0)
    all_values = jnp.concatenate([page_rows[:, :, 1], win_values], axis=0)
    visible = jnp.concatenate([key_page[None, :] == own_page[:, None], win_visible], axis=1)
    weighted, row_max, row_total = attend(query_rows, all_keys, all_values, visible)
    attn = weighted / row_total[..., None]
    attn = attn.astype(jnp.bfloat16).reshape(tok_count, width)
    mixed = jnp.dot(attn, out_weight, preferred_element_type=jnp.float32)
    resid = (hidden_in.astype(jnp.float32) + mixed).astype(jnp.bfloat16)
    normed = rms_scale(resid.astype(jnp.float32), moe_gain).astype(jnp.bfloat16)
    route_flat = routes.reshape(-1)
    slots = slot_numbers(route_flat, experts)
    place = route_flat * capacity + slots
    token_ids = jnp.arange(tok_count * TOP, dtype=jnp.int32) // TOP
    slot_tokens = jnp.full((experts * capacity,), tok_count, jnp.int32).at[place].set(token_ids)
    padded_rows = jnp.concatenate([normed, jnp.zeros((1, width), jnp.bfloat16)], axis=0)
    outgoing = padded_rows[slot_tokens].reshape(experts, capacity, width)
    doubled = jnp.broadcast_to(outgoing[:, None], (experts, 2, capacity, width)).reshape(
        2 * experts, capacity, width
    )
    arrived = lax.all_to_all(doubled, ("req", "exp"), split_axis=0, concat_axis=0, tiled=True)
    partial_value = expert_piece(arrived, gate_weight, up_weight, down_weight)
    returned = lax.all_to_all(
        partial_value, ("req", "exp"), split_axis=0, concat_axis=0, tiled=True
    ).reshape(experts, 2, capacity, width)
    results = (returned[:, 0].astype(jnp.float32) + returned[:, 1].astype(jnp.float32)).astype(
        jnp.bfloat16
    )
    picked = results.reshape(experts * capacity, width)[place].reshape(tok_count, TOP, width)
    combined = jnp.einsum("tk,tkd->td", route_weight, picked.astype(jnp.float32))
    layer_out = (resid.astype(jnp.float32) + combined).astype(jnp.bfloat16)
    token_score = jnp.dot(
        layer_out.astype(jnp.float32), score_weight, precision=lax.Precision.HIGHEST
    )
    doc_partial = jnp.dot(
        token_score, own_member.astype(jnp.float32), precision=lax.Precision.HIGHEST
    )
    doc_sums = lax.psum(doc_partial, "exp")
    doc_scores = (doc_sums / doc_len.astype(jnp.float32))[None, :]
    return (layer_out, doc_scores)


def solution(mesh):
    in_specs = (
        P(("req", "exp"), None),
        P(("req", "exp"), None),
        P(),
        P(),
        P("req", None, None, "exp"),
        P("req", None),
        P("req", None),
        P("req", None),
        P(),
        P(),
        P(("req", "exp"), None),
        P(("req", "exp"), None),
        P(("req", "exp"), None, None),
        P(("req", "exp"), None, None),
        P(("req", "exp"), None, None),
        P(),
    )
    out_specs = (P(("req", "exp"), None), P("req", None))
    return jax.shard_map(local, mesh=mesh, in_specs=in_specs, out_specs=out_specs, check_vma=False)
```

profile of v0, /device:TPU:0, one launch (start us, length us, event | category | flops | bytes accessed | tf_op | source)
XLA Modules:
  0.0 650.3 jit_solution(14052082231563304019)
XLA Ops:
  7.3 0.7 all-gather.3.cloned.1.call-update
  8.0 0.7 copy.44
  8.8 0.1 reduce
  8.9 0.5 slice.72
  9.4 2.5 fusion.57
  11.9 0.3 copy.64
  12.2 1.2 copy.43
  13.4 1.3 copy.66
  14.7 1.3 copy.48
  16.1 0.7 and_select_fusion.1
  16.9 0.1 multiply_reduce_fusion.1
  17.0 0.1 multiply_reduce_fusion.2
  17.2 0.3 multiply_cosine_fusion
  17.5 1.9 multiply_multiply_fusion
  19.4 1.7 subtract_convert_fusion
  21.1 0.3 pad_maximum_fusion.2
  21.4 0.3 copy.45
  21.7 1.4 copy.65
  23.1 1.1 pad_maximum_fusion.1
  24.2 4.9 collective-permute-start
  29.1 1.3 collective-permute-start.1
  30.4 0.1 copy.52
  30.7 0.7 fusion.39
  31.4 30.8 %reduce-window.11 = s32[64,8,128]{2,1,0:T(8,128)S(1)} reduce-window(s32[64,8,128]{2,1,0:T(8,128)} %fusion.39, s32[]{:T(128)} %constant.72.clone.1), window={size=1x1x128 pad=0_0x0_0x127_0}, to_apply=%region_11.12 | reduce-window | flops 8323072 | bytes 524292 | tf_op jit(solution)/shard_map/reduce-window.1
  62.2 0.8 slice.79
  63.1 1.1 copy.54
  64.3 0.1 copy.51
  64.4 0.1 mul.211
  64.5 0.1 broadcast_add_fusion
  64.7 4.6 scatter_custom_fusion
  69.6 0.6 and_select_fusion
  70.3 0.1 broadcast_compare_fusion
  70.5 6.6 %pad_maximum_fusion = bf16[384,4096]{0,1:T(8,128)(2,1)S(1)} fusion(bf16[128,4096]{0,1:T(8,128)(2,1)} %collective-permute-done.1, bf16[128,2048]{0,1:T(8,128)(2,1)S(1)} %copy.65, bf16[128,2048]{0,1:T(8,128)(2,1)S(1)} %bitcast.117, bf16[128,4096]{0,1:T(8,128)(2,1)} %collective-permute-done), kind=kLoop, calls=%fused_computation.27 | loop fusion | flops 12582912 | bytes 6291456 | tf_op jit(solution)/shard_map/concatenate | solution.py:27
  77.1 2.1 fusion.56
  79.2 2.6 copy.50
  81.8 32.5 %all-gather.3.cloned.1.call-done = bf16[1,8,128,4096]{3,2,1,0:T(8,128)(2,1)} async-done(((bf16[1,8,128,256]{3,2,1,0:T(8,128)(2,1)}), bf16[1,8,128,4096]{3,2,1,0:T(8,128)(2,1)}) %all-gather.3.cloned.1.call-update) | async-done | bytes 8388624 | tf_op jit(solution)/shard_map/all_gather | solution.py:153
  114.3 14.3 %reshape.297 = bf16[1024,16,2,128]{3,2,1,0:T(2,128)(2,1)} reshape(bf16[1,8,128,4096]{3,2,1,0:T(8,128)(2,1)} %all-gather.3.cloned.1.call-done) | data formatting | bytes 16777216 | tf_op jit(solution)/shard_map/reshape | solution.py:153
  128.6 17.2 %fusion.55 = (bf16[1024,16,1,128]{3,2,1,0:T(2,128)(2,1)}, bf16[1024,16,1,128]{3,2,1,0:T(2,128)(2,1)S(1)}) fusion(bf16[1024,16,2,128]{3,2,1,0:T(2,128)(2,1)} %reshape.297), kind=kLoop, calls=%fused_computation.114 | loop fusion | bytes 16777216 | tf_op jit(solution)/shard_map/slice | solution.py:157
  145.8 4.7 copy.74
  150.6 20.1 %copy.63 = bf16[1024,16,1,128]{0,3,1,2:T(8,128)(2,1)} copy(bf16[1024,16,1,128]{3,2,1,0:T(2,128)(2,1)} %get-tuple-element.4) | data formatting | bytes 8388608
  170.7 9.0 %fusion.6 = f32[16,128,1408]{2,1,0:T(8,128)} fusion(bf16[384,16,128]{2,0,1:T(8,128)(2,1)} %copy.50, bf16[1024,16,128]{2,0,1:T(8,128)(2,1)} %bitcast.109, bf16[128,16,64]{2,0,1:T(8,128)(2,1)S(1)} %copy-done.5, bf16[128,16,64]{2,0,1:T(8,128)(2,1)S(1)} %copy-done.4), kind=kOutput, calls=%fused_computation.16 | convolution fusion | flops 750780416 | bytes 17825792 | tf_op jit(solution)/shard_map/nhd,khd->hnk/dot_general | solution.py:75
  179.7 14.6 %fusion.58 = (f32[16,128]{1,0:T(8,128)S(1)}, bf16[16,128,1408]{2,1,0:T(8,128)(2,1)}) fusion(f32[16,128,1408]{2,1,0:T(8,128)} %fusion.6, pred[128,1408]{1,0:T(8,128)(4,1)S(1)} %pad_add_fusion), kind=kOutput, calls=%fused_computation.117 | output fusion | flops 23070080 | bytes 17489920 | tf_op jit(solution)/shard_map/sub | solution.py:80
  194.3 6.3 divide_convert_fusion
  200.7 2.4 multiply_reduce_fusion
  203.1 1.0 copy-done.2
  204.1 0.2 multiply_convert_fusion.1
  204.3 7.1 %gather_fusion = bf16[1536,2048]{1,0:T(8,128)(2,1)} fusion(bf16[129,2048]{1,0:T(8,128)(2,1)S(1)} %concatenate.33, s32[2048]{0:T(1024)S(1)} %pad_clamp_fusion), kind=kCustom, calls=%fused_computation | custom fusion | bytes 12589056 | tf_op jit(solution)/shard_map/gather | solution.py:171
  211.4 5.2 broadcast_in_dim.129
  216.6 150.9 %all_to_all.10 = bf16[128,24,2048]{2,1,0:T(8,128)(2,1)S(1)} all-to-all(bf16[128,24,2048]{2,1,0:T(8,128)(2,1)S(1)} %bitcast.105), channel_id=1, replica_groups=mesh['req'=8,'exp'=16] {'req','exp'}, dimensions={0} | all-to-all | bytes 25165824 | tf_op jit(solution)/shard_map/all_to_all | solution.py:175
  367.5 4.5 copy-done.1
  372.0 8.7 %fusion.21 = f32[3072,512]{1,0:T(8,128)} fusion(bf16[3072,2048]{1,0:T(8,128)(2,1)S(1)} %bitcast.111, bf16[1,2048,512]{2,1,0:T(8,128)(2,1)S(1)} %copy-done.15), kind=kOutput, calls=%fused_computation.33 | convolution fusion | flops 6442450944 | bytes 20971520 | tf_op jit(solution)/shard_map/dot_general | solution.py:98
  380.7 21.0 %convolution_convert_fusion = bf16[3072,2048]{1,0:T(8,128)(2,1)} fusion(bf16[1,512,2048]{2,1,0:T(8,128)(2,1)S(1)} %copy-done, f32[3072,512]{1,0:T(8,128)} %fusion.21, bf16[3072,2048]{1,0:T(8,128)(2,1)} %bitcast.112, bf16[1,2048,512]{2,1,0:T(8,128)(2,1)} %param.29), kind=kOutput, calls=%fused_computation.7 | convolution fusion | flops 12900630528 | bytes 35651584 | tf_op jit(solution)/shard_map/dot_general | solution.py:101
  401.7 6.3 all-to-all-start.1
  408.0 0.1 copy.58
  408.2 167.8 %all-to-all-done.1 = bf16[128,24,2048]{2,1,0:T(8,128)(2,1)} async-done(((bf16[128,24,2048]{2,1,0:T(8,128)(2,1)}), bf16[128,24,2048]{2,1,0:T(8,128)(2,1)}, u32[]{:S(2)}, u32[]{:S(2)}) %all-to-all-start.1) | async-done | bytes 12582944 | tf_op jit(solution)/shard_map/all_to_all | solution.py:177
  576.0 9.1 %add_convert_fusion = bf16[64,1,24,2048]{3,2,0,1:T(8,128)(2,1)} fusion(bf16[64,2,24,2048]{3,2,1,0:T(8,128)(2,1)} %bitcast.28), kind=kLoop, calls=%fused_computation.4 | loop fusion | flops 12582912 | bytes 18874368 | tf_op jit(solution)/shard_map/convert_element_type | solution.py:180
  585.1 12.5 %gather_fusion.1 = bf16[1024,2048]{1,0:T(8,128)(2,1)} fusion(bf16[1536,2048]{1,0:T(8,128)(2,1)} %bitcast.104, s32[1024]{0:T(1024)S(1)} %broadcast_clamp_fusion), kind=kCustom, calls=%fused_computation.1 | custom fusion | bytes 8392704 | tf_op jit(solution)/shard_map/gather | solution.py:183
  597.6 3.4 fusion.14
  601.1 0.5 fusion.28
  601.6 0.8 copy-done.6
  602.4 0.5 convolution_bitcast_fusion.1
  602.9 0.1 convolution_bitcast_fusion
  603.0 39.6 %psum.7 = f32[32]{0:T(128)S(1)} all-reduce(f32[32]{0:T(128)S(1)} %convolution_bitcast_fusion), channel_id=1, replica_groups=mesh['req'=8,'exp'=16] {'exp'}, use_global_device_ids=true, to_apply=%region_15.16 | all-reduce | flops 32 | bytes 256 | tf_op jit(solution)/shard_map/psum | solution.py:192
  642.7 0.5 fusion.49
  (68 shorter events, 1.2 us)
Async XLA Ops:
  7.2 373.6 %copy-start = (bf16[1,512,2048]{2,1,0:T(8,128)(2,1)S(1)}, bf16[1,512,2048]{2,1,0:T(8,128)(2,1)}, u32[]{:S(2)}) copy-start(bf16[1,512,2048]{2,1,0:T(8,128)(2,1)} %param.30) | copy-start | bytes 6291460
  7.2 9.6 %copy-start.14 = (s32[1,32]{1,0:T(1,128)S(1)}, s32[1,32]{1,0:T(1,128)}, u32[]{:S(2)}) copy-start(s32[1,32]{1,0:T(1,128)} %param.22) | copy-start | bytes 388
  7.2 9.6 %copy-start.13 = (s32[1,32]{1,0:T(1,128)S(1)}, s32[1,32]{1,0:T(1,128)}, u32[]{:S(2)}) copy-start(s32[1,32]{1,0:T(1,128)} %param.23) | copy-start | bytes 388
  7.2 10.3 %copy-start.11 = (f32[128]{0:T(128)S(1)}, f32[128]{0:T(128)}, u32[]{:S(2)}) copy-start(f32[128]{0:T(128)} %param.18) | copy-start | bytes 1540
  7.2 10.3 %copy-start.12 = (f32[128]{0:T(128)S(1)}, f32[128]{0:T(128)}, u32[]{:S(2)}) copy-start(f32[128]{0:T(128)} %param.19) | copy-start | bytes 1540
  7.2 107.0 %all-gather.3.cloned.1.call-start = ((), (), s32[]{:S(2)}) async-start(), calls=%async_computation.2 | async-start | bytes 8912896 | tf_op jit(solution)/shard_map/all_gather | solution.py:153
  19.4 11.0 %copy-start.7 = (s32[128,8]{0,1:T(8,128)S(1)}, s32[128,8]{0,1:T(8,128)}, u32[]{:S(2)}) copy-start(s32[128,8]{0,1:T(8,128)} %param.26) | copy-start | bytes 12292
  19.4 50.0 %copy-start.16 = (s32[1,8]{1,0:T(1,128)S(1)}, s32[1,8]{1,0:T(1,128)}, u32[]{:S(2)}) copy-start(s32[1,8]{1,0:T(1,128)} %param.21) | copy-start | bytes 100
  24.2 46.3 %collective-permute-start = (bf16[128,4096]{0,1:T(8,128)(2,1)}, bf16[128,4096]{0,1:T(8,128)(2,1)}, u32[]{:S(2)}, u32[]{:S(2)}) collective-permute-start(bf16[128,4096]{0,1:T(8,128)(2,1)} %pad_maximum_fusion.1), channel_id=1, source_target_pairs={{0,1},{1,2},{2,3},{3,4},{4,5},{5,6},{6,7},{7,8},{8,9},{9,10},{10,1... | collective-permute-start | bytes 3145736 | tf_op jit(solution)/shard_map/ppermute | solution.py:23
  29.1 41.4 %collective-permute-start.1 = (bf16[128,4096]{0,1:T(8,128)(2,1)}, bf16[128,4096]{0,1:T(8,128)(2,1)}, u32[]{:S(2)}, u32[]{:S(2)}) collective-permute-start(bf16[128,4096]{0,1:T(8,128)(2,1)} %pad_maximum_fusion.1), channel_id=1, source_target_pairs={{1,0},{2,1},{3,2},{4,3},{5,4},{6,5},{7,6},{8,7},{9,8},{10,9},{11,1... | collective-permute-start | bytes 3145736 | tf_op jit(solution)/shard_map/ppermute | solution.py:26
  150.6 20.1 %copy-start.4 = (bf16[128,16,64]{2,0,1:T(8,128)(2,1)S(1)}, bf16[128,16,64]{2,0,1:T(8,128)(2,1)}, u32[]{:S(2)}) copy-start(bf16[128,16,64]{2,0,1:T(8,128)(2,1)} %get-tuple-element.11) | copy-start | bytes 786436
  150.6 20.1 %copy-start.5 = (bf16[128,16,64]{2,0,1:T(8,128)(2,1)S(1)}, bf16[128,16,64]{2,0,1:T(8,128)(2,1)}, u32[]{:S(2)}) copy-start(bf16[128,16,64]{2,0,1:T(8,128)(2,1)} %get-tuple-element.12) | copy-start | bytes 786436
  170.7 29.9 %slice-start = ((s8[8388608]{0:T(1024)(128)(4,1)}), s8[4194304]{0:T(1024)(128)(4,1)S(1)}, s32[]{:S(2)}) async-start(s8[8388608]{0:T(1024)(128)(4,1)} %bitcast.106), calls=%async_computation.3 | async-start | bytes 8388608
  179.7 20.9 %slice-start.1 = ((s8[8388608]{0:T(1024)(128)(4,1)}), s8[4194304]{0:T(1024)(128)(4,1)S(1)}, s32[]{:S(2)}) async-start(s8[8388608]{0:T(1024)(128)(4,1)} %bitcast.106), calls=%async_computation.4 | async-start | bytes 8388608
  200.6 3.4 copy-start.8
  203.1 1.0 copy-start.2
  216.6 155.4 %copy-start.15 = (bf16[1,2048,512]{2,1,0:T(8,128)(2,1)S(1)}, bf16[1,2048,512]{2,1,0:T(8,128)(2,1)}, u32[]{:S(2)}) copy-start(bf16[1,2048,512]{2,1,0:T(8,128)(2,1)} %param.28) | copy-start | bytes 6291460
  367.5 4.5 copy-start.1
  401.7 6.3 copy-start.10
  401.7 174.3 %all-to-all-start.1 = ((bf16[128,24,2048]{2,1,0:T(8,128)(2,1)}), bf16[128,24,2048]{2,1,0:T(8,128)(2,1)}, u32[]{:S(2)}, u32[]{:S(2)}) async-start(bf16[128,24,2048]{2,1,0:T(8,128)(2,1)} %bitcast.110), calls=%async_computation.1 | async-start | bytes 25165824 | tf_op jit(solution)/shard_map/all_to_all | solution.py:177
  585.1 15.9 %copy-start.3 = (f32[128,2048]{1,0:T(8,128)S(1)}, f32[128,2048]{1,0:T(8,128)}, u32[]{:S(2)}) copy-start(f32[128,2048]{1,0:T(8,128)} %copy-done.2) | copy-start | bytes 3145732
  597.6 4.7 copy-start.9
  601.6 0.8 copy-start.6
Sparse Core Ops, SparseCore 0:
  10.2 104.0 all-gather.2
where the time goes:
time: 658 us; the launch traced here: 650 us
  waiting for transfers between devices  201 us (31%)
  blocking collectives  191 us (29%)
  local copies, waits for them, and re-layouts  109 us (17%)
  other arithmetic  71.1 us (11%)
  matrix products  51.5 us (8%)
  between operations  14.8 us (2%)
  starting transfers between devices  12.5 us (2%)
    all_to_all x1, waiting for transfers between devices, local(): lax.all_to_all(partial_value, ('req', 'exp'), split_axis=0, concat_axis=0...  168 us
    all_to_all x1, blocking collectives, local(): lax.all_to_all(doubled, ('req', 'exp'), split_axis=0, concat_axis=0, tile...  151 us
    psum x1, blocking collectives, local(): doc_sums = lax.psum(doc_partial, 'exp')  39.6 us
    unnamed x45, local copies, waits for them, and re-layouts  34.3 us
    another operation x6, other arithmetic  32.9 us
    all_gather x1, waiting for transfers between devices, local(): lax.all_gather(query_pages[0], 'exp', axis=2, tiled=True)  32.5 us
    dot_general x1, matrix products, expert_piece(): jnp.dot(hidden_act, down_weight[0], preferred_element_type=jnp.float32)  21 us
    slice x1, local copies, waits for them, and re-layouts, local(): all_values = jnp.concatenate([page_rows[:, :, 1], win_values], axis=0)  17.2 us
  transfers between devices with their start and end apart: 4, of which 2 were waited for; matrix products, arithmetic and copies ran while one was open for 10% of the time, Pallas kernels for 0%

commit v1 on v0

v1 whole, which is shorter than its diff:
```python
import functools

import jax
import jax.numpy as jnp
import numpy as np
from jax import lax
from jax.experimental import pallas as pl
from jax.experimental.pallas import tpu as pltpu
from jax.sharding import PartitionSpec as P

D = 2048
HEADS = 16
HD = 128
FFH = 512
TOK = 128
DOCS = 32
NQ = 8
PAGE = 128
CAP = 24
LINE = 4
ROWS = LINE * CAP
PLANE = 16
NCH = 4
CH = D // NCH
EPS = 1e-06
ROPE_BASE = 50000.0
NEG = -1e30

F32 = jnp.float32
BF16 = jnp.bfloat16
MESH = pl.DeviceIdType.MESH


def iota(shape, dim):
    return lax.broadcasted_iota(jnp.int32, shape, dim)


def iota_f(shape, dim):
    return iota(shape, dim).astype(F32)


def kernel(
    hidden, qkv, q_gain, k_gain, pages, page_table, doc_len, doc_query, w_out, moe_gain, meta,
    gate_w, up_w, down_w, score_w, freq,
    lay, doc_out,
    head_stage, head_all, attn, attn_stage, wo_buf, gate_b, up_b, down_b, meta_all, tri, rank,
    wrow, sel, wsel, resid, tok, stage, arrive, act, ret, part, part_stage, part_in, dsum,
    head_s, head_r, attn_s, attn_r, wo_sem, meta_s, meta_r, loc_sem, wa_s, wa_r, wb_s, wb_r,
    tok_s, tok_r, disp_s, disp_r, ret_s, ret_r, part_s, part_r, dsum_s, dsum_r,
):
    req = lax.axis_index("req")
    me = lax.axis_index("exp")
    y, core = req // 2, req % 2
    x, z = me // 4, me % 4
    kappa = core == z % 2

    def peer(px, py, pz, pc):
        return (2 * py + pc, 4 * px + pz)

    sibling = (2 * y + (1 - core), me)
    partner = (req, 4 * x + (z + 1 - 2 * (z % 2)))

    barrier = pltpu.get_barrier_semaphore()

    @pl.loop(1, 16)
    def _(i):
        pl.semaphore_signal(barrier, 1, device_id=(req, (me + i) % 16), device_id_type=MESH)

    @pl.loop(1, 4)
    def _(dy):
        @pl.loop(0, 4)
        def _(dx):
            pl.semaphore_signal(
                barrier, 1, device_id=peer((x + dx) % 4, (y + dy) % 4, z, core), device_id_type=MESH
            )

    pl.semaphore_signal(barrier, 1, device_id=sibling, device_id_type=MESH)
    pl.semaphore_wait(barrier, 28)

    def remote(src, dst, send, recv, device):
        return pltpu.make_async_remote_copy(
            src_ref=src, dst_ref=dst, send_sem=send, recv_sem=recv, device_id=device, device_id_type=MESH
        )

    def meta_copy(dz):
        return remote(
            meta_all.at[z], meta_all.at[z], meta_s.at[dz - 1], meta_r.at[dz - 1],
            peer(x, y, (z + dz) % 4, core),
        )

    meta_all[z] = meta[...]
    for dz in range(1, 4):
        meta_copy(dz).start()

    def wo_copy(n):
        return pltpu.make_async_copy(
            w_out.at[:, pl.ds(n * CH, CH)], wo_buf.at[n % 2], wo_sem.at[n % 2]
        )

    wo_copy(0).start()
    wo_copy(1).start()

    len_row = doc_len[...].astype(F32)
    eye = iota((DOCS, DOCS), 0) == iota((DOCS, DOCS), 1)
    len_col = jnp.sum(jnp.where(eye, len_row, 0.0), axis=1, keepdims=True)
    upto = iota((DOCS, DOCS), 0) <= iota((DOCS, DOCS), 1)
    ends = jnp.sum(jnp.where(upto, len_col, 0.0), axis=0, keepdims=True)
    starts = ends - len_row
    eye_q = iota((NQ, NQ), 0) == iota((NQ, NQ), 1)
    page_col = jnp.sum(
        jnp.where(eye_q, page_table[...].astype(F32), 0.0), axis=1, keepdims=True
    )
    page_row = jnp.sum(
        jnp.where(doc_query[...] == iota((NQ, DOCS), 0), page_col, 0.0), axis=0, keepdims=True
    )

    def positions(block):
        return (block * TOK).astype(F32) + iota_f((TOK, 1), 0)

    own_pos = positions(me)
    own_start = jnp.max(jnp.where(starts <= own_pos, starts, 0.0), axis=1, keepdims=True)
    angles = (PAGE + own_pos - own_start) * freq[...]
    cosine = jnp.cos(angles)
    sine = jnp.sin(angles)
    sine = jnp.where(iota((TOK, HD), 1) < HD // 2, -sine, sine)

    def norm_rope(values, gain):
        values = values.astype(F32)
        mean_sq = jnp.mean(values * values, axis=-1, keepdims=True)
        values = values * lax.rsqrt(mean_sq + EPS) * gain[...]
        return (values * cosine + pltpu.roll(values, HD // 2, 1) * sine).astype(BF16)

    def head_copy(head):
        return remote(
            head_stage.at[head], head_all.at[me], head_s.at[head], head_r.at[me], (req, head)
        )

    @pl.loop(1, 17)
    def _(i):
        head = (me + i) % 16
        col = pl.multiple_of(head * HD, HD)
        head_stage[head, :, 0:HD] = norm_rope(qkv[:, pl.ds(col, HD)], q_gain)
        head_stage[head, :, HD : 2 * HD] = norm_rope(qkv[:, pl.ds(D + col, HD)], k_gain)
        head_stage[head, :, 2 * HD : 3 * HD] = qkv[:, pl.ds(2 * D + col, HD)]

        @pl.when(i < 16)
        def _():
            head_copy(head).start()

    head_all[me] = head_stage[me]

    weights = ((gate_w, gate_b), (up_w, up_b), (down_w, down_b))

    def local_weight(n):
        return pltpu.make_async_copy(weights[n][0].at[0], weights[n][1].at[0], loc_sem.at[n])

    def first_weight(n):
        return remote(
            weights[n][0].at[0], weights[n][1].at[0], wa_s.at[n], wa_r.at[n], sibling
        )

    def cross_weight(n):
        return remote(
            weights[n][0].at[0], weights[n][1].at[1], wa_s.at[n], wb_r.at[n], partner
        )

    def second_weight(n):
        return remote(
            weights[n][1].at[1], weights[n][1].at[1], wb_s.at[n], wb_r.at[n], sibling
        )

    @pl.when(kappa)
    def _():
        for n in range(3):
            local_weight(n).start()
            first_weight(n).start()

    @pl.when(jnp.logical_not(kappa))
    def _():
        for n in range(3):
            cross_weight(n).start()

    for dz in range(1, 4):
        src = (z - dz + 4) % 4
        remote(
            meta_all.at[src], meta_all.at[src], meta_s.at[dz - 1], meta_r.at[dz - 1], sibling
        ).wait_recv()
    slot = iota((PLANE, 1), 0)
    to_x = (slot % 4 + x) % 4
    to_y = (slot % 4 + slot // 4 + y) % 4
    expert = ((2 * to_y + z % 2) * 8 + 2 * to_x + z // 2).astype(F32)
    for j in range(LINE):
        mask = jnp.zeros((PLANE, TOK), F32)
        weight = jnp.zeros((PLANE, TOK), F32)
        for n in range(8):
            hit = meta_all[j, n : n + 1, :] == expert
            mask = jnp.where(hit, 1.0, mask)
            weight = jnp.where(hit, meta_all[j, 8 + n : 9 + n, :], weight)
        rank[:, j * TOK : (j + 1) * TOK] = mask
        wrow[:, j * TOK : (j + 1) * TOK] = weight
    tri[...] = jnp.where(
        iota((LINE * TOK, LINE * TOK), 0) < iota((LINE * TOK, LINE * TOK), 1), 1.0, 0.0
    ).astype(BF16)
    mask = rank[...]
    prior = jnp.dot(mask.astype(BF16), tri[...], preferred_element_type=F32)
    rank[...] = jnp.where(mask > 0.0, prior, -1.0)

    @pl.loop(0, PLANE)
    def _(r):
        hit = rank[pl.ds(r, 1), :] == iota_f((ROWS, LINE * TOK), 0)
        rows = pl.ds(pl.multiple_of(r * ROWS, ROWS), ROWS)
        sel[rows, :] = jnp.where(hit, 1.0, 0.0).astype(BF16)
        wsel[rows, :] = jnp.where(hit, wrow[pl.ds(r, 1), :], 0.0).astype(BF16)

    @pl.loop(1, 16)
    def _(i):
        src = (me - i + 16) % 16
        remote(
            head_stage.at[src], head_all.at[src], head_s.at[src], head_r.at[src], sibling
        ).wait_recv()

    page_keys = pages[:, :, 0:HD].reshape(NQ * PAGE, HD)
    page_values = pages[:, :, HD : 2 * HD].reshape(NQ * PAGE, HD)
    my_col = pl.ds(pl.multiple_of(me * HD, HD), HD)

    def attn_copy(block):
        return remote(
            attn_stage.at[block], attn.at[:, my_col], attn_s.at[block], attn_r.at[me], (req, block)
        )

    contract_last = (((1,), (1,)), ((), ()))

    @pl.loop(1, 17)
    def _(i):
        block = (me + i) % 16
        first = jnp.clip(block - 1, 0, 13)
        query = head_all[block, :, 0:HD]
        keys = head_all[pl.ds(first, 3), :, HD : 2 * HD].reshape(3 * TOK, HD)
        values = head_all[pl.ds(first, 3), :, 2 * HD : 3 * HD].reshape(3 * TOK, HD)
        pos = positions(block)
        began = starts <= pos
        left = ends > pos
        start = jnp.max(jnp.where(began, starts, 0.0), axis=1, keepdims=True)
        end = jnp.min(jnp.where(left, ends, 4096.0), axis=1, keepdims=True)
        page = jnp.sum(jnp.where(began & left, page_row, 0.0), axis=1, keepdims=True)
        scale = HD**-0.5
        near = lax.dot_general(query, keys, contract_last, preferred_element_type=F32) * scale
        paged = lax.dot_general(query, page_keys, contract_last, preferred_element_type=F32)
        own = paged[:, 0:PAGE]
        for n in range(1, NQ):
            own = jnp.where(page == float(n), paged[:, n * PAGE : (n + 1) * PAGE], own)
        own = own * scale
        key_pos = (first * TOK).astype(F32) + iota_f((TOK, 3 * TOK), 1)
        visible = (key_pos >= start) & (key_pos < end)
        near = jnp.where(visible, near, NEG)
        top = jnp.maximum(
            jnp.max(near, axis=1, keepdims=True), jnp.max(own, axis=1, keepdims=True)
        )
        near = jnp.where(visible, jnp.exp(near - top), 0.0)
        own = jnp.exp(own - top)
        total = jnp.sum(near, axis=1, keepdims=True) + jnp.sum(own, axis=1, keepdims=True)
        spread = jnp.concatenate(
            [jnp.where(page == float(n), own, 0.0).astype(BF16) for n in range(NQ)], axis=1
        )
        weighted = jnp.dot(near.astype(BF16), values, preferred_element_type=F32)
        weighted = weighted + jnp.dot(spread, page_values, preferred_element_type=F32)
        attn_stage[block] = (weighted / total).astype(BF16)

        @pl.when(i < 16)
        def _():
            attn_copy(block).start()

    attn[:, my_col] = attn_stage[me]

    @pl.loop(1, 16)
    def _(i):
        src = (me - i + 16) % 16
        col = pl.ds(pl.multiple_of(src * HD, HD), HD)
        remote(
            attn_stage.at[src], attn.at[:, col], attn_s.at[src], attn_r.at[src], sibling
        ).wait_recv()

    square = jnp.zeros((TOK, 1), F32)
    for n in range(NCH):
        cols = slice(n * CH, (n + 1) * CH)
        wo_copy(n).wait()
        mixed = jnp.dot(attn[...], wo_buf[n % 2], preferred_element_type=F32)
        summed = (hidden[:, cols].astype(F32) + mixed).astype(BF16)
        resid[:, cols] = summed
        wide = summed.astype(F32)
        square = square + jnp.sum(wide * wide, axis=1, keepdims=True)
        if n + 2 < NCH:
            wo_copy(n + 2).start()
    inverse = lax.rsqrt(square * (1.0 / D) + EPS)
    my_rows = pl.ds(pl.multiple_of(z * TOK, TOK), TOK)

    def tok_copy(c, dz):
        block = tok.at[my_rows, pl.ds(c * CH, CH)]
        return remote(
            block, block, tok_s.at[c, dz - 1], tok_r.at[c, dz - 1], peer(x, y, (z + dz) % 4, core)
        )

    for c in range(NCH):
        cols = slice(c * CH, (c + 1) * CH)
        tok[my_rows, cols] = (resid[:, cols].astype(F32) * inverse * moe_gain[:, cols]).astype(BF16)
        for dz in range(1, 4):
            tok_copy(c, dz).start()

    def row_block(r):
        return pl.ds(pl.multiple_of(r * ROWS, ROWS), ROWS)

    def disp_copy(g, i, c):
        rows = row_block(g * 4 + i)
        cols = pl.ds(c * CH, CH)
        return remote(
            stage.at[rows, cols], arrive.at[rows, cols],
            disp_s.at[g * 4 + i, c], disp_r.at[g * 4 + i, c],
            peer((x + i) % 4, (y + i + g) % 4, z, core),
        )

    def select_rows(g, c):
        rows = pl.ds(pl.multiple_of(g * 4 * ROWS, 4 * ROWS), 4 * ROWS)
        cols = slice(c * CH, (c + 1) * CH)
        picked = jnp.dot(sel[rows, :], tok[:, cols], preferred_element_type=F32)
        stage[rows, cols] = picked.astype(BF16)

    for c in range(NCH):
        cols = slice(c * CH, (c + 1) * CH)
        for dz in range(1, 4):
            rows = pl.ds(pl.multiple_of(((z - dz + 4) % 4) * TOK, TOK), TOK)
            block = tok.at[rows, pl.ds(c * CH, CH)]
            remote(block, block, tok_s.at[c, dz - 1], tok_r.at[c, dz - 1], sibling).wait_recv()
        select_rows(0, c)
        for i in range(1, 4):
            disp_copy(0, i, c).start()
        arrive[0:ROWS, cols] = stage[0:ROWS, cols]

    @pl.loop(1, 4)
    def _(g):
        for c in range(NCH):
            select_rows(g, c)
            for i in range(4):
                disp_copy(g, i, c).start()

    @pl.when(kappa)
    def _():
        for n in range(3):
            cross_weight(n).wait_recv()
            second_weight(n).start()
        for n in range(3):
            local_weight(n).wait()

    @pl.when(jnp.logical_not(kappa))
    def _():
        for n in range(3):
            first_weight(n).wait_recv()
            second_weight(n).wait_recv()

    @pl.loop(0, 4)
    def _(g):
        for i in range(4):
            if i == 0:
                @pl.when(g > 0)
                def _():
                    for c in range(NCH):
                        disp_copy(g, 0, c).wait_recv()
            else:
                for c in range(NCH):
                    disp_copy(g, i, c).wait_recv()
        rows = pl.ds(pl.multiple_of(g * 4 * ROWS, 4 * ROWS), 4 * ROWS)
        for s in range(2):
            gate = jnp.dot(arrive[rows, :], gate_b[s], preferred_element_type=F32)
            up = jnp.dot(arrive[rows, :], up_b[s], preferred_element_type=F32)
            act[rows, s * FFH : (s + 1) * FFH] = (
                gate * (1.0 / (1.0 + jnp.exp(-gate))) * up
            ).astype(BF16)

    def ret_copy(g, i, c):
        rows = row_block(g * 4 + i)
        cols = pl.ds(c * CH, CH)
        return remote(
            arrive.at[rows, cols], ret.at[rows, cols],
            ret_s.at[g * 4 + i, c], ret_r.at[g * 4 + i, c],
            peer((x - i + 4) % 4, (y - i - g + 8) % 4, z, core),
        )

    for c in range(NCH):
        cols = slice(c * CH, (c + 1) * CH)

        @pl.loop(0, 4)
        def _(g):
            rows = pl.ds(pl.multiple_of(g * 4 * ROWS, 4 * ROWS), 4 * ROWS)
            piece = jnp.dot(act[rows, 0:FFH], down_b[0, :, cols], preferred_element_type=F32)
            piece = piece + jnp.dot(
                act[rows, FFH : 2 * FFH], down_b[1, :, cols], preferred_element_type=F32
            )
            arrive[rows, cols] = piece.astype(BF16)
            for i in range(4):
                if i == 0:
                    @pl.when(g > 0)
                    def _():
                        ret_copy(g, 0, c).start()
                else:
                    ret_copy(g, i, c).start()

        ret[0:ROWS, cols] = arrive[0:ROWS, cols]

    def part_copy(c, dz):
        target = (z + dz) % 4
        rows = pl.ds(pl.multiple_of(target * TOK, TOK), TOK)
        return remote(
            part_stage.at[c, rows, :], part_in.at[c, dz - 1],
            part_s.at[c, dz - 1], part_r.at[c, dz - 1], peer(x, y, target, core),
        )

    def combine(c):
        cols = slice(c * CH, (c + 1) * CH)

        @pl.loop(0, 4)
        def _(g):
            for i in range(4):
                if i == 0:
                    @pl.when(g > 0)
                    def _():
                        ret_copy(g, 0, c).wait_recv()
                else:
                    ret_copy(g, i, c).wait_recv()

        sums = lax.dot_general(
            wsel[...], ret[:, cols], (((0,), (0,)), ((), ())), preferred_element_type=F32
        )
        part_stage[c] = sums.astype(BF16)
        for dz in range(1, 4):
            part_copy(c, dz).start()
        part[...] = sums
        return part[my_rows, :]

    def finish(c, own, score):
        cols = slice(c * CH, (c + 1) * CH)
        total = own
        for dz in range(1, 4):
            part_copy(c, dz).wait_recv()
            total = total + part_in[c, dz - 1].astype(F32)
        out = (resid[:, cols].astype(F32) + total).astype(BF16)
        lay[:, cols] = out
        return score + jnp.sum(out.astype(F32) * score_w[:, cols], axis=1, keepdims=True)

    score = jnp.zeros((TOK, 1), F32)
    for c in range(NCH):
        tok_own = combine(c)
        own_sums = tok_own
        if c > 0:
            score = finish(c - 1, previous, score)
        previous = own_sums
    score = finish(NCH - 1, previous, score)

    member = (starts <= own_pos) & (ends > own_pos)
    sums = jnp.sum(jnp.where(member, score, 0.0), axis=0, keepdims=True)
    dsum[me, :, 0:DOCS] = jnp.broadcast_to(sums, (8, DOCS))
    dsum[me, :, DOCS:128] = jnp.zeros((8, 128 - DOCS), F32)

    def dsum_copy(target):
        return remote(dsum.at[me], dsum.at[me], dsum_s.at[target], dsum_r.at[me], (req, target))

    @pl.loop(1, 16)
    def _(i):
        dsum_copy((me + i) % 16).start()

    for dz in range(1, 4):
        meta_copy(dz).wait_send()
    for n in range(3):
        @pl.when(kappa)
        def _():
            first_weight(n).wait_send()
            second_weight(n).wait_send()

        @pl.when(jnp.logical_not(kappa))
        def _():
            cross_weight(n).wait_send()

    @pl.loop(1, 16)
    def _(i):
        head_copy((me + i) % 16).wait_send()
        attn_copy((me + i) % 16).wait_send()

    for c in range(NCH):
        for dz in range(1, 4):
            tok_copy(c, dz).wait_send()
            part_copy(c, dz).wait_send()

        @pl.loop(0, 4)
        def _(g):
            for i in range(4):
                if i == 0:
                    @pl.when(g > 0)
                    def _():
                        disp_copy(g, 0, c).wait_send()
                        ret_copy(g, 0, c).wait_send()
                else:
                    disp_copy(g, i, c).wait_send()
                    ret_copy(g, i, c).wait_send()

    @pl.loop(1, 16)
    def _(i):
        src = (me - i + 16) % 16
        remote(
            dsum.at[src], dsum.at[src], dsum_s.at[src], dsum_r.at[src], sibling
        ).wait_recv()

    whole = dsum[0]
    for n in range(1, 16):
        whole = whole + dsum[n]
    doc_out[...] = whole[0:1, 0:DOCS] / len_row

    @pl.loop(1, 16)
    def _(i):
        dsum_copy((me + i) % 16).wait_send()


def local(
    hidden_in, qkv, q_gain, k_gain, query_pages, page_table, doc_lengths, doc_query, out_weight,
    moe_gain, routes, route_weight, gate_weight, up_weight, down_weight, score_weight,
):
    meta = jnp.concatenate([routes.T.astype(F32), route_weight.T], axis=0)
    half = ROPE_BASE ** (-(np.arange(HD // 2, dtype=np.float32) * 2.0 / HD))
    freq = jnp.asarray(np.concatenate([half, half])[None].astype(np.float32))
    vmem = pl.BlockSpec(memory_space=pltpu.VMEM)
    hbm = pl.BlockSpec(memory_space=pl.ANY)
    dma = pltpu.SemaphoreType.DMA
    call = pl.pallas_call(
        kernel,
        out_shape=(
            jax.ShapeDtypeStruct((TOK, D), BF16),
            jax.ShapeDtypeStruct((1, DOCS), F32),
        ),
        in_specs=[
            vmem, vmem, vmem, vmem, vmem, vmem, vmem, vmem, hbm, vmem, vmem,
            hbm, hbm, hbm, vmem, vmem,
        ],
        out_specs=(vmem, vmem),
        scratch_shapes=[
            pltpu.VMEM((HEADS, TOK, 3 * HD), BF16),
            pltpu.VMEM((HEADS, TOK, 3 * HD), BF16),
            pltpu.VMEM((TOK, D), BF16),
            pltpu.VMEM((HEADS, TOK, HD), BF16),
            pltpu.VMEM((2, D, CH), BF16),
            pltpu.VMEM((2, D, FFH), BF16),
            pltpu.VMEM((2, D, FFH), BF16),
            pltpu.VMEM((2, FFH, D), BF16),
            pltpu.VMEM((LINE, 16, TOK), F32),
            pltpu.VMEM((LINE * TOK, LINE * TOK), BF16),
            pltpu.VMEM((PLANE, LINE * TOK), F32),
            pltpu.VMEM((PLANE, LINE * TOK), F32),
            pltpu.VMEM((PLANE * ROWS, LINE * TOK), BF16),
            pltpu.VMEM((PLANE * ROWS, LINE * TOK), BF16),
            pltpu.VMEM((TOK, D), BF16),
            pltpu.VMEM((LINE * TOK, D), BF16),
            pltpu.VMEM((PLANE * ROWS, D), BF16),
            pltpu.VMEM((PLANE * ROWS, D), BF16),
            pltpu.VMEM((PLANE * ROWS, 2 * FFH), BF16),
            pltpu.VMEM((PLANE * ROWS, D), BF16),
            pltpu.VMEM((LINE * TOK, CH), F32),
            pltpu.VMEM((NCH, LINE * TOK, CH), BF16),
            pltpu.VMEM((NCH, LINE - 1, TOK, CH), BF16),
            pltpu.VMEM((16, 8, 128), F32),
            dma((16,)), dma((16,)), dma((16,)), dma((16,)), dma((2,)),
            dma((3,)), dma((3,)), dma((3,)), dma((3,)), dma((3,)), dma((3,)), dma((3,)),
            dma((NCH, 3)), dma((NCH, 3)),
            dma((PLANE, NCH)), dma((PLANE, NCH)), dma((PLANE, NCH)), dma((PLANE, NCH)),
            dma((NCH, 3)), dma((NCH, 3)), dma((16,)), dma((16,)),
        ],
        compiler_params=pltpu.CompilerParams(
            collective_id=0, has_side_effects=True, vmem_limit_bytes=60 * 1024 * 1024
        ),
        cost_estimate=pl.CostEstimate(
            flops=26_000_000_000, bytes_accessed=20_000_000, transcendentals=3_000_000
        ),
    )
    return call(
        hidden_in, qkv, q_gain[None], k_gain[None], query_pages[0], page_table, doc_lengths,
        doc_query, out_weight, moe_gain[None], meta, gate_weight, up_weight, down_weight,
        score_weight[None], freq,
    )


def solution(mesh):
    rows = P(("req", "exp"), None)
    blocks = P(("req", "exp"), None, None)
    in_specs = (
        rows, rows, P(), P(), P("req", None, None, "exp"), P("req", None), P("req", None),
        P("req", None), P(), P(), rows, rows, blocks, blocks, blocks, P(),
    )
    out_specs = (rows, P("req", None))
    return jax.shard_map(local, mesh=mesh, in_specs=in_specs, out_specs=out_specs, check_vma=False)
```

time: 658 us -> 301 us (0.46); the launches traced: 650 us -> 301 us
  Pallas kernels: 0 us -> 295 us
  waiting for transfers between devices: 201 us -> 0 us
  blocking collectives: 191 us -> 0 us
  local copies, waits for them, and re-layouts: 109 us -> 2.99 us
  other arithmetic: 71.1 us -> 1.98 us
  matrix products: 51.5 us -> 0 us
  between operations: 14.8 us -> 0.64 us
  starting transfers between devices: 12.5 us -> 0 us
    pallas_call x0 -> x1, Pallas kernels: none -> 295 us  [local(): call(hidden_in, qkv, q_gain[None], k_gain[None], query_pages[0], page_tab...]
    all_to_all x1 -> x0, waiting for transfers between devices: 168 us -> none  [local(): lax.all_to_all(partial_value, ('req', 'exp'), split_axis=0, concat_axis=0...]
    all_to_all x1 -> x0, blocking collectives: 151 us -> none  [local(): lax.all_to_all(doubled, ('req', 'exp'), split_axis=0, concat_axis=0, tile...]
    dot_general x8 -> x0, matrix products: 51.5 us -> none  [the longest x1 21 us: expert_piece(): jnp.dot(hidden_act, down_weight[0], preferred_element_type=jnp.float32)]
    psum x1 -> x0, blocking collectives: 39.6 us -> none  [local(): doc_sums = lax.psum(doc_partial, 'exp')]
    another operation x6 -> x0, other arithmetic: 32.9 us -> none
    all_gather x1 -> x0, waiting for transfers between devices: 32.5 us -> none  [local(): lax.all_gather(query_pages[0], 'exp', axis=2, tiled=True)]
    unnamed x45 -> x2, local copies, waits for them, and re-layouts: 34.3 us -> 2.99 us
  transfers between devices with their start and end apart: 4 -> 0, of which waited for: 2 -> 0; matrix products, arithmetic and copies ran while one was open for 10% -> 0% of each run, Pallas kernels for 0% -> 0%
where the time goes in v1:
time: 301 us
  Pallas kernels  295 us (98%)
    pallas_call x1, Pallas kernels, local(): call(hidden_in, qkv, q_gain[None], k_gain[None], query_pages[0], page_tab...  295 us

profile of v1, /device:TPU:0, one launch (start us, length us, event | category | flops | bytes accessed | tf_op | source)
XLA Modules:
  0.0 300.6 jit_solution(5549774801287154583)
XLA Ops:
  0.6 0.7 convert_bitcast_fusion
  1.3 1.3 pad_maximum_fusion.meta
  2.6 295.0 %shard_map.176 = (bf16[128,2048]{1,0:T(8,128)(2,1)}, f32[1,32]{1,0:T(1,128)}) custom-call(bf16[128,2048]{1,0:T(8,128)(2,1)} %hidden.1, bf16[128,6144]{1,0:T(8,128)(2,1)} %qkv.1, f32[1,128]{1,0:T(1,128)} %bitcast.12, f32[1,128]{1,0:T(1,128)} %bitcast.13, bf16[8,128,256]{2,1,0:T(8,128)(2,1)} %bitcast.9, s32[1,8]{1,0:T(1,128)} %page_table.1, s32[1,32]{1,0:T(1,128)} %doc_len.1, ...), custom_call_target="tpu_custom_call" | custom-call | flops 25999998976 | bytes 20000000 | tf_op jit(solution)/shard_map/pallas_call | solution.py:579
  297.7 1.9 copy.21
  299.5 1.1 copy.22

commit v2 on v1

--- a/solution.py
+++ b/solution.py
@@ -26,6 +26,15 @@
 ROPE_BASE = 50000.0
 NEG = -1e30
 
+OFFSETS = (
+    (1, 2), (3, 2), (2, 1), (2, 3),
+    (1, 3), (3, 1), (2, 0), (0, 2),
+    (0, 0), (2, 2), (1, 1), (3, 3),
+    (1, 0), (3, 0), (0, 1), (0, 3),
+)
+SELF = OFFSETS.index((0, 0))
+OTHERS_THEN_SELF = OFFSETS[:SELF] + OFFSETS[SELF + 1 :] + OFFSETS[SELF : SELF + 1]
+
 F32 = jnp.float32
 BF16 = jnp.bfloat16
 MESH = pl.DeviceIdType.MESH
@@ -39,8 +48,17 @@
     return iota(shape, dim).astype(F32)
 
 
+def pick(table, axis, index):
+    if isinstance(index, int):
+        return table[index][axis]
+    value = table[-1][axis]
+    for n in range(len(table) - 1):
+        value = jnp.where(index == n, table[n][axis], value)
+    return value
+
+
 def kernel(
-    hidden, qkv, q_gain, k_gain, pages, page_table, doc_len, doc_query, w_out, moe_gain, meta,
+    hidden, qkv, q_gain, k_gain, pages, page_table, doc_len, doc_query, w_out, moe_gain, routes, route_w,
     gate_w, up_w, down_w, score_w, freq,
     lay, doc_out,
     head_stage, head_all, attn, attn_stage, wo_buf, gate_b, up_b, down_b, meta_all, tri, rank,
@@ -82,13 +100,41 @@
             src_ref=src, dst_ref=dst, send_sem=send, recv_sem=recv, device_id=device, device_id_type=MESH
         )
 
+    weights = ((gate_w, gate_b), (up_w, up_b), (down_w, down_b))
+
+    def local_weight(n):
+        return pltpu.make_async_copy(weights[n][0].at[0], weights[n][1].at[0], loc_sem.at[n])
+
+    def first_weight(n):
+        return remote(
+            weights[n][0].at[0], weights[n][1].at[0], wa_s.at[n], wa_r.at[n], sibling
+        )
+
+    def cross_weight(n):
+        return remote(
+            weights[n][0].at[0], weights[n][1].at[1], wa_s.at[n], wb_r.at[n], partner
+        )
+
+    def second_weight(n):
+        return remote(
+            weights[n][1].at[1], weights[n][1].at[1], wb_s.at[n], wb_r.at[n], sibling
+        )
+
     def meta_copy(dz):
         return remote(
             meta_all.at[z], meta_all.at[z], meta_s.at[dz - 1], meta_r.at[dz - 1],
             peer(x, y, (z + dz) % 4, core),
         )
 
-    meta_all[z] = meta[...]
+    identity = jnp.where(iota((TOK, TOK), 0) == iota((TOK, TOK), 1), 1.0, 0.0).astype(BF16)
+
+    def turned(values):
+        return lax.dot_general(
+            values.astype(BF16), identity, (((0,), (0,)), ((), ())), preferred_element_type=F32
+        )
+
+    meta_all[z, 0:8, :] = turned(routes[...].astype(F32))
+    meta_all[z, 8:16, :] = turned(route_w[...])
     for dz in range(1, 4):
         meta_copy(dz).start()
 
@@ -135,50 +181,28 @@
             head_stage.at[head], head_all.at[me], head_s.at[head], head_r.at[me], (req, head)
         )
 
-    @pl.loop(1, 17)
-    def _(i):
-        head = (me + i) % 16
+    def plane_member(i):
+        return 4 * ((x + pick(OTHERS_THEN_SELF, 0, i)) % 4) + (z + pick(OTHERS_THEN_SELF, 1, i)) % 4
+
+    @pl.loop(0, 16)
+    def _(i):
+        head = plane_member(i)
         col = pl.multiple_of(head * HD, HD)
         head_stage[head, :, 0:HD] = norm_rope(qkv[:, pl.ds(col, HD)], q_gain)
         head_stage[head, :, HD : 2 * HD] = norm_rope(qkv[:, pl.ds(D + col, HD)], k_gain)
         head_stage[head, :, 2 * HD : 3 * HD] = qkv[:, pl.ds(2 * D + col, HD)]
 
-        @pl.when(i < 16)
+        @pl.when(i < 15)
         def _():
             head_copy(head).start()
 
     head_all[me] = head_stage[me]
-
-    weights = ((gate_w, gate_b), (up_w, up_b), (down_w, down_b))
-
-    def local_weight(n):
-        return pltpu.make_async_copy(weights[n][0].at[0], weights[n][1].at[0], loc_sem.at[n])
-
-    def first_weight(n):
-        return remote(
-            weights[n][0].at[0], weights[n][1].at[0], wa_s.at[n], wa_r.at[n], sibling
-        )
-
-    def cross_weight(n):
-        return remote(
-            weights[n][0].at[0], weights[n][1].at[1], wa_s.at[n], wb_r.at[n], partner
-        )
-
-    def second_weight(n):
-        return remote(
-            weights[n][1].at[1], weights[n][1].at[1], wb_s.at[n], wb_r.at[n], sibling
-        )
 
     @pl.when(kappa)
     def _():
         for n in range(3):
             local_weight(n).start()
             first_weight(n).start()
-
-    @pl.when(jnp.logical_not(kappa))
-    def _():
-        for n in range(3):
-            cross_weight(n).start()
 
     for dz in range(1, 4):
         src = (z - dz + 4) % 4
@@ -186,8 +210,8 @@
             meta_all.at[src], meta_all.at[src], meta_s.at[dz - 1], meta_r.at[dz - 1], sibling
         ).wait_recv()
     slot = iota((PLANE, 1), 0)
-    to_x = (slot % 4 + x) % 4
-    to_y = (slot % 4 + slot // 4 + y) % 4
+    to_x = (pick(OFFSETS, 0, slot) + x) % 4
+    to_y = (pick(OFFSETS, 1, slot) + y) % 4
     expert = ((2 * to_y + z % 2) * 8 + 2 * to_x + z // 2).astype(F32)
     for j in range(LINE):
         mask = jnp.zeros((PLANE, TOK), F32)
@@ -230,9 +254,9 @@
 
     contract_last = (((1,), (1,)), ((), ()))
 
-    @pl.loop(1, 17)
-    def _(i):
-        block = (me + i) % 16
+    @pl.loop(0, 16)
+    def _(i):
+        block = plane_member(i)
         first = jnp.clip(block - 1, 0, 13)
         query = head_all[block, :, 0:HD]
         keys = head_all[pl.ds(first, 3), :, HD : 2 * HD].reshape(3 * TOK, HD)
@@ -266,7 +290,7 @@
         weighted = weighted + jnp.dot(spread, page_values, preferred_element_type=F32)
         attn_stage[block] = (weighted / total).astype(BF16)
 
-        @pl.when(i < 16)
+        @pl.when(i < 15)
         def _():
             attn_copy(block).start()
 
@@ -303,19 +327,23 @@
     for c in range(NCH):
         cols = slice(c * CH, (c + 1) * CH)
         tok[my_rows, cols] = (resid[:, cols].astype(F32) * inverse * moe_gain[:, cols]).astype(BF16)
-        for dz in range(1, 4):
+        for dz in (1, 3, 2):
             tok_copy(c, dz).start()
+
+    @pl.when(jnp.logical_not(kappa))
+    def _():
+        for n in range(3):
+            cross_weight(n).start()
 
     def row_block(r):
         return pl.ds(pl.multiple_of(r * ROWS, ROWS), ROWS)
 
-    def disp_copy(g, i, c):
-        rows = row_block(g * 4 + i)
+    def disp_copy(r, c):
+        rows = row_block(r)
         cols = pl.ds(c * CH, CH)
         return remote(
-            stage.at[rows, cols], arrive.at[rows, cols],
-            disp_s.at[g * 4 + i, c], disp_r.at[g * 4 + i, c],
-            peer((x + i) % 4, (y + i + g) % 4, z, core),
+            stage.at[rows, cols], arrive.at[rows, cols], disp_s.at[r, c], disp_r.at[r, c],
+            peer((x + pick(OFFSETS, 0, r)) % 4, (y + pick(OFFSETS, 1, r)) % 4, z, core),
         )
 
     def select_rows(g, c):
@@ -323,6 +351,21 @@
         cols = slice(c * CH, (c + 1) * CH)
         picked = jnp.dot(sel[rows, :], tok[:, cols], preferred_element_type=F32)
         stage[rows, cols] = picked.astype(BF16)
+
+    def not_self(r, action):
+        if isinstance(r, int):
+            if r != SELF:
+                action()
+        else:
+            pl.when(r != SELF)(action)
+
+    def disp_group(g, act_on):
+        for i in range(4):
+            def action(r=g * 4 + i):
+                for c in range(NCH):
+                    act_on(disp_copy(r, c))
+
+            not_self(g * 4 + i, action)
 
     for c in range(NCH):
         cols = slice(c * CH, (c + 1) * CH)
@@ -331,42 +374,45 @@
             block = tok.at[rows, pl.ds(c * CH, CH)]
             remote(block, block, tok_s.at[c, dz - 1], tok_r.at[c, dz - 1], sibling).wait_recv()
         select_rows(0, c)
-        for i in range(1, 4):
-            disp_copy(0, i, c).start()
-        arrive[0:ROWS, cols] = stage[0:ROWS, cols]
+        for i in range(4):
+            disp_copy(i, c).start()
 
     @pl.loop(1, 4)
     def _(g):
         for c in range(NCH):
             select_rows(g, c)
             for i in range(4):
-                disp_copy(g, i, c).start()
-
-    @pl.when(kappa)
-    def _():
-        for n in range(3):
+                not_self(g * 4 + i, lambda r=g * 4 + i: disp_copy(r, c).start())
+
+    self_rows = slice(SELF * ROWS, (SELF + 1) * ROWS)
+    arrive[self_rows, :] = stage[self_rows, :]
+
+    def near_weight(n):
+        @pl.when(kappa)
+        def _():
+            local_weight(n).wait()
+
+        @pl.when(jnp.logical_not(kappa))
+        def _():
+            first_weight(n).wait_recv()
+
+    def far_weight(n):
+        @pl.when(kappa)
+        def _():
             cross_weight(n).wait_recv()
             second_weight(n).start()
-        for n in range(3):
-            local_weight(n).wait()
-
-    @pl.when(jnp.logical_not(kappa))
-    def _():
-        for n in range(3):
-            first_weight(n).wait_recv()
+
+        @pl.when(jnp.logical_not(kappa))
+        def _():
             second_weight(n).wait_recv()
+
+    for n in range(2):
+        near_weight(n)
+        far_weight(n)
 
     @pl.loop(0, 4)
     def _(g):
-        for i in range(4):
-            if i == 0:
-                @pl.when(g > 0)
-                def _():
-                    for c in range(NCH):
-                        disp_copy(g, 0, c).wait_recv()
-            else:
-                for c in range(NCH):
-                    disp_copy(g, i, c).wait_recv()
+        disp_group(g, lambda copy: copy.wait_recv())
         rows = pl.ds(pl.multiple_of(g * 4 * ROWS, 4 * ROWS), 4 * ROWS)
         for s in range(2):
             gate = jnp.dot(arrive[rows, :], gate_b[s], preferred_element_type=F32)
@@ -375,16 +421,20 @@
                 gate * (1.0 / (1.0 + jnp.exp(-gate))) * up
             ).astype(BF16)
 
-    def ret_copy(g, i, c):
-        rows = row_block(g * 4 + i)
+    def ret_copy(r, c):
+        rows = row_block(r)
         cols = pl.ds(c * CH, CH)
         return remote(
-            arrive.at[rows, cols], ret.at[rows, cols],
-            ret_s.at[g * 4 + i, c], ret_r.at[g * 4 + i, c],
-            peer((x - i + 4) % 4, (y - i - g + 8) % 4, z, core),
-        )
-
-    for c in range(NCH):
+            arrive.at[rows, cols], ret.at[rows, cols], ret_s.at[r, c], ret_r.at[r, c],
+            peer((x - pick(OFFSETS, 0, r) + 4) % 4, (y - pick(OFFSETS, 1, r) + 4) % 4, z, core),
+        )
+
+    def ret_chunk(c, act_on):
+        @pl.loop(0, PLANE)
+        def _(r):
+            not_self(r, lambda: act_on(ret_copy(r, c)))
+
+    def down_rows(c):
         cols = slice(c * CH, (c + 1) * CH)
 
         @pl.loop(0, 4)
@@ -395,15 +445,8 @@
                 act[rows, FFH : 2 * FFH], down_b[1, :, cols], preferred_element_type=F32
             )
             arrive[rows, cols] = piece.astype(BF16)
-            for i in range(4):
-                if i == 0:
-                    @pl.when(g > 0)
-                    def _():
-                        ret_copy(g, 0, c).start()
-                else:
-                    ret_copy(g, i, c).start()
-
-        ret[0:ROWS, cols] = arrive[0:ROWS, cols]
+
+        ret[self_rows, cols] = arrive[self_rows, cols]
 
     def part_copy(c, dz):
         target = (z + dz) % 4
@@ -416,21 +459,12 @@
     def combine(c):
         cols = slice(c * CH, (c + 1) * CH)
 
-        @pl.loop(0, 4)
-        def _(g):
-            for i in range(4):
-                if i == 0:
-                    @pl.when(g > 0)
-                    def _():
-                        ret_copy(g, 0, c).wait_recv()
-                else:
-                    ret_copy(g, i, c).wait_recv()
-
+        ret_chunk(c, lambda copy: copy.wait_recv())
         sums = lax.dot_general(
             wsel[...], ret[:, cols], (((0,), (0,)), ((), ())), preferred_element_type=F32
         )
         part_stage[c] = sums.astype(BF16)
-        for dz in range(1, 4):
+        for dz in (1, 3, 2):
             part_copy(c, dz).start()
         part[...] = sums
         return part[my_rows, :]
@@ -445,14 +479,33 @@
         lay[:, cols] = out
         return score + jnp.sum(out.astype(F32) * score_w[:, cols], axis=1, keepdims=True)
 
+    def send_back(c):
+        ret_chunk(c, lambda copy: copy.start())
+
+    def sent_back(c):
+        ret_chunk(c, lambda copy: copy.wait_send())
+
+    near_weight(2)
+    far_weight(2)
     score = jnp.zeros((TOK, 1), F32)
-    for c in range(NCH):
-        tok_own = combine(c)
-        own_sums = tok_own
-        if c > 0:
-            score = finish(c - 1, previous, score)
-        previous = own_sums
-    score = finish(NCH - 1, previous, score)
+    down_rows(0)
+    send_back(0)
+    down_rows(1)
+    send_back(1)
+    down_rows(2)
+    sent_back(0)
+    send_back(2)
+    own_0 = combine(0)
+    down_rows(3)
+    sent_back(1)
+    send_back(3)
+    own_1 = combine(1)
+    score = finish(0, own_0, score)
+    own_2 = combine(2)
+    score = finish(1, own_1, score)
+    own_3 = combine(3)
+    score = finish(2, own_2, score)
+    score = finish(3, own_3, score)
 
     member = (starts <= own_pos) & (ends > own_pos)
     sums = jnp.sum(jnp.where(member, score, 0.0), axis=0, keepdims=True)
@@ -488,17 +541,12 @@
             tok_copy(c, dz).wait_send()
             part_copy(c, dz).wait_send()
 
-        @pl.loop(0, 4)
-        def _(g):
-            for i in range(4):
-                if i == 0:
-                    @pl.when(g > 0)
-                    def _():
-                        disp_copy(g, 0, c).wait_send()
-                        ret_copy(g, 0, c).wait_send()
-                else:
-                    disp_copy(g, i, c).wait_send()
-                    ret_copy(g, i, c).wait_send()
+    @pl.loop(0, 4)
+    def _(g):
+        disp_group(g, lambda copy: copy.wait_send())
+
+    sent_back(2)
+    sent_back(3)
 
     @pl.loop(1, 16)
     def _(i):
@@ -521,7 +569,6 @@
     hidden_in, qkv, q_gain, k_gain, query_pages, page_table, doc_lengths, doc_query, out_weight,
     moe_gain, routes, route_weight, gate_weight, up_weight, down_weight, score_weight,
 ):
-    meta = jnp.concatenate([routes.T.astype(F32), route_weight.T], axis=0)
     half = ROPE_BASE ** (-(np.arange(HD // 2, dtype=np.float32) * 2.0 / HD))
     freq = jnp.asarray(np.concatenate([half, half])[None].astype(np.float32))
     vmem = pl.BlockSpec(memory_space=pltpu.VMEM)
@@ -534,7 +581,7 @@
             jax.ShapeDtypeStruct((1, DOCS), F32),
         ),
         in_specs=[
-            vmem, vmem, vmem, vmem, vmem, vmem, vmem, vmem, hbm, vmem, vmem,
+            vmem, vmem, vmem, vmem, vmem, vmem, vmem, vmem, hbm, vmem, vmem, vmem,
             hbm, hbm, hbm, vmem, vmem,
         ],
         out_specs=(vmem, vmem),
@@ -578,7 +625,7 @@
     )
     return call(
         hidden_in, qkv, q_gain[None], k_gain[None], query_pages[0], page_table, doc_lengths,
-        doc_query, out_weight, moe_gain[None], meta, gate_weight, up_weight, down_weight,
+        doc_query, out_weight, moe_gain[None], routes, route_weight, gate_weight, up_weight, down_weight,
         score_weight[None], freq,
     )
 

time: 301 us -> 239 us (0.79)
  Pallas kernels: 295 us -> 232 us
    pallas_call x1, Pallas kernels: 295 us -> 232 us  [local(): call(hidden_in, qkv, q_gain[None], k_gain[None], query_pages[0], page_tab...]
where the time goes in v2:
time: 239 us
  Pallas kernels  232 us (97%)
  local copies, waits for them, and re-layouts  5.89 us (2%)
    pallas_call x1, Pallas kernels, local(): call(hidden_in, qkv, q_gain[None], k_gain[None], query_pages[0], page_tab...  232 us
    unnamed x4, local copies, waits for them, and re-layouts  5.89 us

profile of v2, /device:TPU:0, one launch (start us, length us, event | category | flops | bytes accessed | tf_op | source)
XLA Modules:
  0.0 238.8 jit_solution(4694750794584494849)
XLA Ops:
  0.6 1.4 copy.19.routes
  2.0 1.4 copy.20.route_w
  3.5 232.3 %shard_map.176 = (bf16[128,2048]{1,0:T(8,128)(2,1)}, f32[1,32]{1,0:T(1,128)}) custom-call(bf16[128,2048]{1,0:T(8,128)(2,1)} %hidden.1, bf16[128,6144]{1,0:T(8,128)(2,1)} %qkv.1, f32[1,128]{1,0:T(1,128)} %bitcast.8, f32[1,128]{1,0:T(1,128)} %bitcast.9, bf16[8,128,256]{2,1,0:T(8,128)(2,1)} %bitcast.5, s32[1,8]{1,0:T(1,128)} %page_table.1, s32[1,32]{1,0:T(1,128)} %doc_len.1, ...), custom_call_target="tpu_custom_call" | custom-call | flops 25999998976 | bytes 20000000 | tf_op jit(solution)/shard_map/pallas_call | solution.py:626
  235.7 1.9 copy.23
  237.6 1.2 copy.24

commit v3 on v2

--- a/solution.py
+++ b/solution.py
@@ -318,17 +318,29 @@
     inverse = lax.rsqrt(square * (1.0 / D) + EPS)
     my_rows = pl.ds(pl.multiple_of(z * TOK, TOK), TOK)
 
-    def tok_copy(c, dz):
-        block = tok.at[my_rows, pl.ds(c * CH, CH)]
-        return remote(
-            block, block, tok_s.at[c, dz - 1], tok_r.at[c, dz - 1], peer(x, y, (z + dz) % 4, core)
-        )
+    mate = z + 1 - 2 * (z % 2)
+    across = 3 - z
+
+    def tok_copy(c, hop):
+        owner = mate if hop == 2 else z
+        rows = pl.ds(pl.multiple_of(owner * TOK, TOK), TOK)
+        block = tok.at[rows, pl.ds(c * CH, CH)]
+        return remote(
+            block, block, tok_s.at[c, hop], tok_r.at[c, hop],
+            peer(x, y, mate if hop == 0 else across, core),
+        )
+
+    def tok_arrival(c, hop):
+        owner = (mate, across, 3 - mate)[hop]
+        rows = pl.ds(pl.multiple_of(owner * TOK, TOK), TOK)
+        block = tok.at[rows, pl.ds(c * CH, CH)]
+        remote(block, block, tok_s.at[c, hop], tok_r.at[c, hop], sibling).wait_recv()
 
     for c in range(NCH):
         cols = slice(c * CH, (c + 1) * CH)
         tok[my_rows, cols] = (resid[:, cols].astype(F32) * inverse * moe_gain[:, cols]).astype(BF16)
-        for dz in (1, 3, 2):
-            tok_copy(c, dz).start()
+        tok_copy(c, 0).start()
+        tok_copy(c, 1).start()
 
     @pl.when(jnp.logical_not(kappa))
     def _():
@@ -369,10 +381,10 @@
 
     for c in range(NCH):
         cols = slice(c * CH, (c + 1) * CH)
-        for dz in range(1, 4):
-            rows = pl.ds(pl.multiple_of(((z - dz + 4) % 4) * TOK, TOK), TOK)
-            block = tok.at[rows, pl.ds(c * CH, CH)]
-            remote(block, block, tok_s.at[c, dz - 1], tok_r.at[c, dz - 1], sibling).wait_recv()
+        tok_arrival(c, 0)
+        tok_copy(c, 2).start()
+        tok_arrival(c, 1)
+        tok_arrival(c, 2)
         select_rows(0, c)
         for i in range(4):
             disp_copy(i, c).start()
@@ -537,9 +549,9 @@
         attn_copy((me + i) % 16).wait_send()
 
     for c in range(NCH):
-        for dz in range(1, 4):
-            tok_copy(c, dz).wait_send()
-            part_copy(c, dz).wait_send()
+        for n in range(3):
+            tok_copy(c, n).wait_send()
+            part_copy(c, n + 1).wait_send()
 
     @pl.loop(0, 4)
     def _(g):

time: 239 us -> 237 us (level); the launches traced: 239 us -> 234 us
  Pallas kernels: 232 us -> 228 us
    pallas_call x1, Pallas kernels: 232 us -> 228 us  [local(): call(hidden_in, qkv, q_gain[None], k_gain[None], query_pages[0], page_tab...]
where the time goes in v3:
time: 237 us; the launch traced here: 234 us
  Pallas kernels  228 us (96%)
  local copies, waits for them, and re-layouts  5.89 us (2%)
    pallas_call x1, Pallas kernels, local(): call(hidden_in, qkv, q_gain[None], k_gain[None], query_pages[0], page_tab...  228 us
    unnamed x4, local copies, waits for them, and re-layouts  5.89 us

profile of v3, /device:TPU:0, one launch (start us, length us, event | category | flops | bytes accessed | tf_op | source)
XLA Modules:
  0.0 234.2 jit_solution(9688407742458924754)
XLA Ops:
  0.6 1.4 copy.19.routes
  2.0 1.4 copy.20.route_w
  3.5 227.7 %shard_map.176 = (bf16[128,2048]{1,0:T(8,128)(2,1)}, f32[1,32]{1,0:T(1,128)}) custom-call(bf16[128,2048]{1,0:T(8,128)(2,1)} %hidden.1, bf16[128,6144]{1,0:T(8,128)(2,1)} %qkv.1, f32[1,128]{1,0:T(1,128)} %bitcast.8, f32[1,128]{1,0:T(1,128)} %bitcast.9, bf16[8,128,256]{2,1,0:T(8,128)(2,1)} %bitcast.5, s32[1,8]{1,0:T(1,128)} %page_table.1, s32[1,32]{1,0:T(1,128)} %doc_len.1, ...), custom_call_target="tpu_custom_call" | custom-call | flops 25999998976 | bytes 20000000 | tf_op jit(solution)/shard_map/pallas_call | solution.py:638
  231.2 1.9 copy.23
  233.0 1.2 copy.24

commit v4 on v3

--- a/solution.py
+++ b/solution.py
@@ -22,6 +22,8 @@
 PLANE = 16
 NCH = 4
 CH = D // NCH
+NWO = 4
+WO = D // NWO
 EPS = 1e-06
 ROPE_BASE = 50000.0
 NEG = -1e30
@@ -140,11 +142,11 @@
 
     def wo_copy(n):
         return pltpu.make_async_copy(
-            w_out.at[:, pl.ds(n * CH, CH)], wo_buf.at[n % 2], wo_sem.at[n % 2]
-        )
-
-    wo_copy(0).start()
-    wo_copy(1).start()
+            w_out.at[:, pl.ds(n * WO, WO)], wo_buf.at[n % 3], wo_sem.at[n % 3]
+        )
+
+    for n in range(3):
+        wo_copy(n).start()
 
     len_row = doc_len[...].astype(F32)
     eye = iota((DOCS, DOCS), 0) == iota((DOCS, DOCS), 1)
@@ -305,16 +307,16 @@
         ).wait_recv()
 
     square = jnp.zeros((TOK, 1), F32)
-    for n in range(NCH):
-        cols = slice(n * CH, (n + 1) * CH)
+    for n in range(NWO):
+        cols = slice(n * WO, (n + 1) * WO)
         wo_copy(n).wait()
-        mixed = jnp.dot(attn[...], wo_buf[n % 2], preferred_element_type=F32)
+        mixed = jnp.dot(attn[...], wo_buf[n % 3], preferred_element_type=F32)
         summed = (hidden[:, cols].astype(F32) + mixed).astype(BF16)
         resid[:, cols] = summed
         wide = summed.astype(F32)
         square = square + jnp.sum(wide * wide, axis=1, keepdims=True)
-        if n + 2 < NCH:
-            wo_copy(n + 2).start()
+        if n + 3 < NWO:
+            wo_copy(n + 3).start()
     inverse = lax.rsqrt(square * (1.0 / D) + EPS)
     my_rows = pl.ds(pl.multiple_of(z * TOK, TOK), TOK)
 
@@ -322,12 +324,12 @@
     across = 3 - z
 
     def tok_copy(c, hop):
-        owner = mate if hop == 2 else z
+        owner = mate if hop == 2 and c > 0 else z
         rows = pl.ds(pl.multiple_of(owner * TOK, TOK), TOK)
         block = tok.at[rows, pl.ds(c * CH, CH)]
         return remote(
             block, block, tok_s.at[c, hop], tok_r.at[c, hop],
-            peer(x, y, mate if hop == 0 else across, core),
+            peer(x, y, (mate, across, across if c > 0 else (z + 2) % 4)[hop], core),
         )
 
     def tok_arrival(c, hop):
@@ -339,8 +341,8 @@
     for c in range(NCH):
         cols = slice(c * CH, (c + 1) * CH)
         tok[my_rows, cols] = (resid[:, cols].astype(F32) * inverse * moe_gain[:, cols]).astype(BF16)
-        tok_copy(c, 0).start()
-        tok_copy(c, 1).start()
+        for hop in range(3 if c == 0 else 2):
+            tok_copy(c, hop).start()
 
     @pl.when(jnp.logical_not(kappa))
     def _():
@@ -382,7 +384,8 @@
     for c in range(NCH):
         cols = slice(c * CH, (c + 1) * CH)
         tok_arrival(c, 0)
-        tok_copy(c, 2).start()
+        if c > 0:
+            tok_copy(c, 2).start()
         tok_arrival(c, 1)
         tok_arrival(c, 2)
         select_rows(0, c)
@@ -500,24 +503,17 @@
     near_weight(2)
     far_weight(2)
     score = jnp.zeros((TOK, 1), F32)
-    down_rows(0)
-    send_back(0)
-    down_rows(1)
-    send_back(1)
-    down_rows(2)
-    sent_back(0)
-    send_back(2)
-    own_0 = combine(0)
-    down_rows(3)
-    sent_back(1)
-    send_back(3)
-    own_1 = combine(1)
-    score = finish(0, own_0, score)
-    own_2 = combine(2)
-    score = finish(1, own_1, score)
-    own_3 = combine(3)
-    score = finish(2, own_2, score)
-    score = finish(3, own_3, score)
+    own = {}
+    for step in range(NCH + 3):
+        if step < NCH:
+            down_rows(step)
+            if step >= 2:
+                sent_back(step - 2)
+            send_back(step)
+        if 2 <= step < NCH + 2:
+            own[step - 2] = combine(step - 2)
+        if step >= 3:
+            score = finish(step - 3, own.pop(step - 3), score)
 
     member = (starts <= own_pos) & (ends > own_pos)
     sums = jnp.sum(jnp.where(member, score, 0.0), axis=0, keepdims=True)
@@ -557,8 +553,8 @@
     def _(g):
         disp_group(g, lambda copy: copy.wait_send())
 
-    sent_back(2)
-    sent_back(3)
+    sent_back(NCH - 2)
+    sent_back(NCH - 1)
 
     @pl.loop(1, 16)
     def _(i):
@@ -602,7 +598,7 @@
             pltpu.VMEM((HEADS, TOK, 3 * HD), BF16),
             pltpu.VMEM((TOK, D), BF16),
             pltpu.VMEM((HEADS, TOK, HD), BF16),
-            pltpu.VMEM((2, D, CH), BF16),
+            pltpu.VMEM((3, D, WO), BF16),
             pltpu.VMEM((2, D, FFH), BF16),
             pltpu.VMEM((2, D, FFH), BF16),
             pltpu.VMEM((2, FFH, D), BF16),
@@ -622,7 +618,7 @@
             pltpu.VMEM((NCH, LINE * TOK, CH), BF16),
             pltpu.VMEM((NCH, LINE - 1, TOK, CH), BF16),
             pltpu.VMEM((16, 8, 128), F32),
-            dma((16,)), dma((16,)), dma((16,)), dma((16,)), dma((2,)),
+            dma((16,)), dma((16,)), dma((16,)), dma((16,)), dma((3,)),
             dma((3,)), dma((3,)), dma((3,)), dma((3,)), dma((3,)), dma((3,)), dma((3,)),
             dma((NCH, 3)), dma((NCH, 3)),
             dma((PLANE, NCH)), dma((PLANE, NCH)), dma((PLANE, NCH)), dma((PLANE, NCH)),

time: 237 us -> 232 us (0.979)
  Pallas kernels: 228 us -> 223 us
    pallas_call x1, Pallas kernels: 228 us -> 223 us  [local(): call(hidden_in, qkv, q_gain[None], k_gain[None], query_pages[0], page_tab...]
where the time goes in v4:
time: 232 us; the launch traced here: 230 us
  Pallas kernels  223 us (96%)
  local copies, waits for them, and re-layouts  5.89 us (3%)
    pallas_call x1, Pallas kernels, local(): call(hidden_in, qkv, q_gain[None], k_gain[None], query_pages[0], page_tab...  223 us
    unnamed x4, local copies, waits for them, and re-layouts  5.89 us

profile of v4, /device:TPU:0, one launch (start us, length us, event | category | flops | bytes accessed | tf_op | source)
XLA Modules:
  0.0 230.0 jit_solution(14268293423293736392)
XLA Ops:
  0.6 1.4 copy.19.routes
  2.0 1.4 copy.20.route_w
  3.5 223.4 %shard_map.176 = (bf16[128,2048]{1,0:T(8,128)(2,1)}, f32[1,32]{1,0:T(1,128)}) custom-call(bf16[128,2048]{1,0:T(8,128)(2,1)} %hidden.1, bf16[128,6144]{1,0:T(8,128)(2,1)} %qkv.1, f32[1,128]{1,0:T(1,128)} %bitcast.8, f32[1,128]{1,0:T(1,128)} %bitcast.9, bf16[8,128,256]{2,1,0:T(8,128)(2,1)} %bitcast.5, s32[1,8]{1,0:T(1,128)} %page_table.1, s32[1,32]{1,0:T(1,128)} %doc_len.1, ...), custom_call_target="tpu_custom_call" | custom-call | flops 25999998976 | bytes 20000000 | tf_op jit(solution)/shard_map/pallas_call | solution.py:634
  226.9 1.9 copy.23
  228.8 1.2 copy.24

commit v5 on v4

--- a/solution.py
+++ b/solution.py
@@ -324,12 +324,12 @@
     across = 3 - z
 
     def tok_copy(c, hop):
-        owner = mate if hop == 2 and c > 0 else z
+        owner = mate if hop == 2 and c > 1 else z
         rows = pl.ds(pl.multiple_of(owner * TOK, TOK), TOK)
         block = tok.at[rows, pl.ds(c * CH, CH)]
         return remote(
             block, block, tok_s.at[c, hop], tok_r.at[c, hop],
-            peer(x, y, (mate, across, across if c > 0 else (z + 2) % 4)[hop], core),
+            peer(x, y, (mate, across, across if c > 1 else (z + 2) % 4)[hop], core),
         )
 
     def tok_arrival(c, hop):
@@ -341,7 +341,7 @@
     for c in range(NCH):
         cols = slice(c * CH, (c + 1) * CH)
         tok[my_rows, cols] = (resid[:, cols].astype(F32) * inverse * moe_gain[:, cols]).astype(BF16)
-        for hop in range(3 if c == 0 else 2):
+        for hop in range(3 if c < 2 else 2):
             tok_copy(c, hop).start()
 
     @pl.when(jnp.logical_not(kappa))
@@ -384,7 +384,7 @@
     for c in range(NCH):
         cols = slice(c * CH, (c + 1) * CH)
         tok_arrival(c, 0)
-        if c > 0:
+        if c > 1:
             tok_copy(c, 2).start()
         tok_arrival(c, 1)
         tok_arrival(c, 2)

time: 232 us -> 233 us (level)
  Pallas kernels: 223 us -> 226 us
    pallas_call x1, Pallas kernels: 223 us -> 226 us  [local(): call(hidden_in, qkv, q_gain[None], k_gain[None], query_pages[0], page_tab...]
where the time goes in v5:
time: 233 us; the launch traced here: 232 us
  Pallas kernels  226 us (97%)
  local copies, waits for them, and re-layouts  5.89 us (3%)
    pallas_call x1, Pallas kernels, local(): call(hidden_in, qkv, q_gain[None], k_gain[None], query_pages[0], page_tab...  226 us
    unnamed x4, local copies, waits for them, and re-layouts  5.89 us

profile of v5, /device:TPU:0, one launch (start us, length us, event | category | flops | bytes accessed | tf_op | source)
XLA Modules:
  0.0 232.4 jit_solution(13277412368260512392)
XLA Ops:
  0.6 1.4 copy.19.routes
  2.0 1.4 copy.20.route_w
  3.5 225.8 %shard_map.176 = (bf16[128,2048]{1,0:T(8,128)(2,1)}, f32[1,32]{1,0:T(1,128)}) custom-call(bf16[128,2048]{1,0:T(8,128)(2,1)} %hidden.1, bf16[128,6144]{1,0:T(8,128)(2,1)} %qkv.1, f32[1,128]{1,0:T(1,128)} %bitcast.8, f32[1,128]{1,0:T(1,128)} %bitcast.9, bf16[8,128,256]{2,1,0:T(8,128)(2,1)} %bitcast.5, s32[1,8]{1,0:T(1,128)} %page_table.1, s32[1,32]{1,0:T(1,128)} %doc_len.1, ...), custom_call_target="tpu_custom_call" | custom-call | flops 25999998976 | bytes 20000000 | tf_op jit(solution)/shard_map/pallas_call | solution.py:634
  229.3 1.9 copy.23
  231.2 1.2 copy.24
